TPU v7x, 32 devices: a whole 2x2x4 slice. The times are simulated.
32 devices in a mesh: cls: 4 (over z), vol: 8 (over y, x, core).
Axes of the slice: x: 2, y: 2, z: 4, core: 2. Of those that a mesh axis runs over, the one named last changes fastest.
Arguments:
- images: bfloat16 [256, 256, 2, 256], P(('cls', 'vol')), may hold values from -8 to 8
- projections: bfloat16 [4, 128, 256, 2, 256], P('cls', None, 'vol'), may hold values from -0.049718446 to 0.049718446
- assignment: int32 [256, 1], P(('cls', 'vol')), may hold values from 0 to 3; in each aligned block of 8 rows (0 to 7, 8 to 15, ...) at most 4 rows name the same one
- interp_cells: int32 [128, 4, 256], replicated, may hold values from 0 to 65535, as said below
- interp_weights: float32 [128, 4, 256], replicated, may hold values from 0 to 1, as said below
Outputs:
- class_volume: float32 [4, 256, 256, 256], P('cls', 'vol')
Inputs may be any that keep to these rules, and one draw needn't show every extreme that they name: `assignment`: among the 8 particles of one device (aligned blocks of 8 rows), at most 4 name the same class. `interp_cells`: for each direction and column u the four cells are (x, y), (x + 1, y), (x, y + 1), (x + 1, y + 1) modulo 256, in that order. `interp_weights`: for each direction and column u the four weights are nonnegative and sum to one.
All inputs are finite; a program needn't handle non-finite values.
Results may differ from a plain program's by a relative error of at most 0.0027.
Values may be sent and summed in bfloat16 or wider, within the bound.
No kernel may reach another device: no remote copies, remote signals or barrier semaphores. Data moves between devices by JAX's collectives and lax.ppermute only.
A program may use at most 256 MiB of HBM per device.

v0:
```python
import functools
import math

import jax
import jax.numpy as jnp
import numpy as np
from jax import lax
from jax.experimental import pallas as pl
from jax.experimental.pallas import tpu as pltpu
from jax.sharding import PartitionSpec as P

F32 = jnp.float32
BF16 = jnp.bfloat16
LANES = 128
HALF = 64
CHUNK = 128
PAD = 8
UNROLL = 8
VMEM = pltpu.VMEM


def split_table(table):
    high = table.astype(jnp.bfloat16)
    low = (table - high.astype(np.float64)).astype(jnp.bfloat16)
    return high, low


def plane_pairs(grid, slabs):
    slab = grid // slabs
    half = slab // 2
    pairs = []
    for w in range(slabs):
        for i in range(half):
            if w < slabs // 2:
                first = slab * w + 1 + i
            else:
                first = slab * w + half - 1 - i
            if 2 * first == grid:
                pairs.append((0, first))
            else:
                pairs.append((first, grid - first))
    return np.array(pairs).reshape(slabs, half, 2)


def tables(grid, slabs):
    half = grid // 2
    scale = 1.0 / math.sqrt(grid)
    index = np.arange(grid)
    angle = 2.0 * np.pi / grid
    phase = (index[:, None] * np.arange(half)[None, :]) % grid
    cosine = np.cos(phase * angle)
    sine = np.sin(phase * angle)
    sine[:, 0] = np.cos(((index * half) % grid) * angle)
    table_y = np.concatenate([cosine, sine], axis=1) * scale
    rows = half + 8
    phase = (np.arange(rows)[:, None] * index[None, :]) % grid
    live = (np.arange(rows) <= half)[:, None]
    table_x = np.concatenate([np.cos(phase * angle) * live, np.sin(phase * angle) * live], axis=0) * scale
    pairs = plane_pairs(grid, slabs).reshape(-1, 2)
    single = (2 * pairs[:, 1] == grid)[:, None]
    z = np.where(single[:, 0], pairs[:, 1], pairs[:, 0])
    phase = (z[:, None] * index[None, :]) % grid
    for_sum = np.where(single, 1.0, np.cos(phase * angle))
    for_difference = np.where(single, np.cos(phase * angle), -np.sin(phase * angle))
    table_z = np.stack([for_sum, for_difference], axis=1).reshape(grid, grid) * scale
    order = np.concatenate([np.arange(half), [half], np.arange(grid - 1, half, -1)])
    restore = (order[None, :] == index[:, None]).astype(jnp.bfloat16)
    return split_table(table_y), split_table(table_x), split_table(table_z), restore


def lane_order(grid, slabs):
    rows = plane_pairs(grid, slabs).transpose(0, 2, 1).reshape(-1)
    source = (2 * rows[:, None] + np.arange(2)[None, :]).reshape(-1)
    return (np.arange(2 * grid)[:, None] == source[None, :]).astype(jnp.bfloat16)


def dot(a, b):
    return jnp.dot(a, b, preferred_element_type=F32)


def dot_t(a, b):
    return lax.dot_general(a, b, (((1,), (1,)), ((), ())), preferred_element_type=F32)


def two_terms(value):
    high = value.astype(BF16)
    low = (value - high.astype(F32)).astype(BF16)
    return high, low


def route_kernel(cap, slabs, width, classes_ref, images_ref, eye_ref, order_ref, out_ref, lines):
    count, _, _, grid = images_ref.shape
    halves = LANES // width
    piece = grid // halves
    lane = lax.broadcasted_iota(jnp.int32, (piece, LANES), 1)
    lines[...] = jnp.zeros_like(lines)

    def place(p, carry):
        own = classes_ref[p, 0]
        rank = 0
        for q in range(count):
            rank = rank + jnp.where((classes_ref[q, 0] == own) & (q < p), 1, 0)
        image = images_ref[p].reshape(-1, grid)
        turned = dot(dot_t(eye_ref[...], image).astype(BF16), order_ref[...])
        for w in range(slabs):
            tile = w * width // LANES * LANES
            block = jnp.zeros((piece, LANES), F32)
            for h in range(halves):
                part = turned[h * piece : (h + 1) * piece, tile : tile + LANES]
                shift = (h * width - (w * width - tile)) % LANES
                part = part if shift == 0 else pltpu.roll(part, shift, 1)
                block = jnp.where((lane >= h * width) & (lane < (h + 1) * width), part, block)
            lines[own * slabs + w, pl.ds(rank, piece, stride=cap), :] = block
        return carry

    lax.fori_loop(0, count, place, 0, unroll=2)
    out_ref[...] = lines[...].astype(BF16).reshape(out_ref.shape)


def route_call(images, assignment, eye, order, class_count, slabs, width, cap):
    count, grid = images.shape[0], images.shape[1]
    rows = grid // (LANES // width) * cap
    vmem = pl.BlockSpec(memory_space=VMEM)
    return pl.pallas_call(
        functools.partial(route_kernel, cap, slabs, width),
        out_shape=jax.ShapeDtypeStruct((class_count * slabs, rows // 16, 16, LANES), BF16),
        in_specs=[pl.BlockSpec(memory_space=pltpu.SMEM)] + [vmem] * 3,
        out_specs=vmem,
        scratch_shapes=[VMEM((class_count * slabs, rows, LANES), F32)],
        compiler_params=pltpu.CompilerParams(vmem_limit_bytes=48 * 2**20),
        name="route",
    )(assignment, images, eye, order)


def score_kernel(cap, dirs, unit, images_ref, kept_ref, joined_ref, out_ref, sums):
    sources, groups, rows16, _ = images_ref.shape
    rows = sources * rows16
    steps = rows16 // cap
    sums[...] = jnp.zeros_like(sums)
    lane = lax.broadcasted_iota(jnp.int32, (steps * dirs, LANES), 1)
    even = (lane & unit) == 0

    def step(g, carry):
        kept = kept_ref[g].astype(F32)
        joined = joined_ref[g].astype(F32)
        refs = [
            jnp.where(even, kept, pltpu.roll(joined, unit, 1)).astype(BF16),
            jnp.where(even, pltpu.roll(kept, LANES - unit, 1), joined).astype(BF16),
        ]
        blocks = [images_ref[:, pl.ds(g + i * (groups // 2), 1), :, :].reshape(rows, LANES) for i in range(2)]
        sums[...] += dot_t(jnp.concatenate(refs, axis=1), jnp.concatenate(blocks, axis=1))
        return carry

    lax.fori_loop(0, groups // 2, step, 0, unroll=2)
    column = lax.broadcasted_iota(jnp.int32, (dirs, rows), 1)
    part = (column & (rows16 - 1)) // cap
    kept = jnp.zeros((dirs, rows), F32)
    for j in range(steps):
        kept = kept + jnp.where(part == j, sums[j * dirs : (j + 1) * dirs, :], 0.0)
    slots = sources * cap
    row_id = lax.broadcasted_iota(jnp.int32, (rows, slots), 0)
    slot_id = lax.broadcasted_iota(jnp.int32, (rows, slots), 1)
    gather = (row_id // rows16 * cap + row_id % cap) == slot_id
    out_ref[...] = jnp.dot(
        kept, gather.astype(F32), preferred_element_type=F32, precision=lax.Precision.HIGHEST
    )


def scores_call(images, kept, joined, cap, dirs, unit):
    sources, groups, rows16, _ = images.shape
    return pl.pallas_call(
        functools.partial(score_kernel, cap, dirs, unit),
        out_shape=jax.ShapeDtypeStruct((dirs, sources * cap), F32),
        in_specs=[pl.BlockSpec(memory_space=VMEM)] * 3,
        out_specs=pl.BlockSpec(memory_space=VMEM),
        scratch_shapes=[VMEM((kept.shape[1], sources * rows16), F32)],
        compiler_params=pltpu.CompilerParams(vmem_limit_bytes=48 * 2**20),
        name="scores",
    )(images, kept, joined)


def scatter_kernel(
    cap,
    width,
    grid,
    turns_ref,
    chunk_row_ref,
    chunk_start_ref,
    chunk_size_ref,
    point_ref,
    parts_ref,
    images_ref,
    weights_ref,
    out_ref,
    values,
    sums,
    spread,
    *buffers,
):
    sources, groups, rows16, _ = images_ref.shape
    rows = sources * rows16
    steps = rows16 // cap
    dirs, slots = parts_ref.shape[1:]
    joined = steps * dirs
    halves = LANES // width

    total = parts_ref[0]
    for i in range(1, parts_ref.shape[0]):
        total = total + parts_ref[i]
    expo = jnp.exp(total - jnp.max(total, axis=0, keepdims=True))
    posterior = (expo / jnp.sum(expo, axis=0, keepdims=True)).astype(BF16)
    slot_id = lax.broadcasted_iota(jnp.int32, (slots, rows), 0)
    row_id = lax.broadcasted_iota(jnp.int32, (slots, rows), 1)
    repeat = ((row_id // rows16 * cap + row_id % cap) == slot_id).astype(F32).astype(BF16)
    wide = dot(posterior, repeat)
    part = (lax.broadcasted_iota(jnp.int32, (dirs, rows), 1) & (rows16 - 1)) // cap
    for j in range(steps):
        spread[j * dirs : (j + 1) * dirs, :] = jnp.where(part == j, wide, 0.0).astype(BF16)

    lane_j = lax.broadcasted_iota(jnp.int32, (joined, LANES), 1)

    def average(g, carry):
        block = images_ref[:, pl.ds(g, 1), :, :].reshape(rows, LANES)
        mean = dot(spread[...], block)
        weight = weights_ref[g]
        for h in range(halves):
            shifted = mean if h == 0 else pltpu.roll(mean, LANES - h * width, 1)
            behind = pltpu.roll(weight, HALF - 8 * h, 1)
            start = pl.multiple_of((h * groups + g) * joined, joined)
            values[pl.ds(start, joined), :] = jnp.where(lane_j < HALF, shifted, behind)
        return carry

    lax.fori_loop(0, groups, average, 0, unroll=2)

    for buffer in buffers:
        buffer[...] = jnp.zeros_like(buffer)
    sums[...] = jnp.zeros_like(sums)

    place = lax.broadcasted_iota(jnp.int32, (CHUNK, LANES), 0)
    lane = lax.broadcasted_iota(jnp.int32, (CHUNK, grid), 1)
    at_y = lane.astype(F32).astype(BF16)
    at_next = ((lane + (grid - 1)) & (grid - 1)).astype(F32).astype(BF16)
    line_8 = lax.broadcasted_iota(jnp.int32, (8, LANES), 0)
    one = jnp.ones((CHUNK, grid), BF16)
    none = jnp.zeros((CHUNK, grid), BF16)

    def fetch(c, buffer):
        start = chunk_start_ref[c]
        for i in range(0, CHUNK, 8):
            block = jnp.broadcast_to(values[pl.ds(point_ref[start + i], 1), :], (8, LANES))
            for j in range(1, 8):
                line = jnp.broadcast_to(values[pl.ds(point_ref[start + i + j], 1), :], (8, LANES))
                block = jnp.where(line_8 == j, line, block)
            buffer[i : i + 8, :] = block

    def put(x, plane):
        for side in range(grid // LANES):
            out_ref[side, pl.ds(x, width, stride=grid + PAD), :] = plane[:, side * LANES : (side + 1) * LANES]

    def work(c, buffer):
        row = chunk_row_ref[c]
        before = chunk_row_ref[jnp.maximum(c - 1, 0)]
        data = buffer[...]
        y = jnp.broadcast_to(data[:, HALF + 4 : HALF + 5], (CHUNK, LANES))
        y = jnp.where(place < chunk_size_ref[c], y, -1.0).astype(BF16)
        y = jnp.concatenate([y] * (grid // LANES), axis=1)
        hot = jnp.concatenate([jnp.where(at_y == y, one, none), jnp.where(at_next == y, one, none)], axis=0)
        turned = data.T
        mean = turned[:width]
        weight = [jnp.broadcast_to(turned[HALF + j : HALF + j + 1], (width, CHUNK)) for j in range(4)]
        operand = jnp.concatenate(
            [
                jnp.concatenate([mean * weight[0], mean * weight[2]], axis=1),
                jnp.concatenate([mean * weight[1], mean * weight[3]], axis=1),
            ],
            axis=0,
        )
        high, low = two_terms(operand)
        result = dot(jnp.concatenate([high, low], axis=0), hot)
        result = result[: 2 * width] + result[2 * width :]
        same = row == before
        old_low, old_high = sums[:width], sums[width:]
        put((before + (grid - 1)) & (grid - 1), old_low)
        sums[:width] = result[:width] + jnp.where(same, old_low, old_high)
        sums[width:] = result[width:] + jnp.where(same, old_high, 0.0)

    fetch(0, buffers[0])

    def several(m, carry):
        for i in range(UNROLL):
            fetch(UNROLL * m + i + 1, buffers[(i + 1) % UNROLL])
            work(UNROLL * m + i, buffers[i])
        return carry

    lax.fori_loop(0, turns_ref[0], several, 0)
    put(grid - 2, sums[:width])
    for side in range(grid // LANES):
        wrapped = pl.ds(grid - 1, width, stride=grid + PAD)
        cut = slice(side * LANES, (side + 1) * LANES)
        out_ref[side, wrapped, :] = out_ref[side, wrapped, :] + sums[width:, cut]


def scatter_call(plan, parts, images, weights, cap, width, grid):
    sources, groups, rows16, _ = images.shape
    dirs = parts.shape[1]
    points = dirs * grid
    smem = pl.BlockSpec(memory_space=pltpu.SMEM)
    vmem = pl.BlockSpec(memory_space=VMEM)
    return pl.pallas_call(
        functools.partial(scatter_kernel, cap, width, grid),
        out_shape=jax.ShapeDtypeStruct((grid // LANES, width * (grid + PAD), LANES), F32),
        in_specs=[smem] * 5 + [vmem] * 3,
        out_specs=vmem,
        scratch_shapes=[
            VMEM((points, LANES), F32),
            VMEM((2 * width, grid), F32),
            VMEM((weights.shape[1], sources * rows16), BF16),
        ]
        + [VMEM((CHUNK, LANES), F32)] * UNROLL,
        compiler_params=pltpu.CompilerParams(vmem_limit_bytes=60 * 2**20),
        name="scatter",
    )(*plan, parts, images, weights)


def plane_kernel(slabs, grid, flag_ref, data_ref, yh_ref, yl_ref, xh_ref, xl_ref, out_ref, lines):
    pairs = data_ref.shape[2] // 2
    half = grid // 2
    rows = half + 8
    slab = grid // slabs
    count = 2 * pairs
    lane = lax.broadcasted_iota(jnp.int32, (grid, half), 1)
    last = (pl.program_id(0) == pl.num_programs(0) - 1) & (flag_ref[0] == 1)

    def along_y(plane):
        high, low = two_terms(plane)
        both = dot(high, yh_ref[...]) + dot(low, yh_ref[...]) + dot(high, yl_ref[...])
        return both[:, :half], both[:, half:]

    def transformed(real, imag):
        cos_r, sin_r = along_y(real)
        cos_i, sin_i = along_y(imag)
        zero_r = jnp.where(lane == 0, 0.0, sin_r)
        zero_i = jnp.where(lane == 0, 0.0, sin_i)
        real = jnp.concatenate([cos_r - zero_i, jnp.where(lane == 0, sin_r, cos_r + sin_i)], axis=1)
        imag = jnp.concatenate([cos_i + zero_r, jnp.where(lane == 0, sin_i, cos_i - sin_r)], axis=1)
        return real, imag

    def along_x(table, operand):
        high, low = operand
        start = table * rows
        upper, lower = xh_ref[start : start + rows], xl_ref[start : start + rows]
        return dot(upper, high) + dot(upper, low) + dot(lower, high)

    def one(i, carry):
        planes = [
            [
                jnp.concatenate([data_ref[part, side, 2 * i + r][:grid] for part in range(grid // LANES)], axis=1)
                for r in range(2)
            ]
            for side in range(2)
        ]
        (a_r, a_i), (b_r, b_i) = planes
        single = last & (i == pairs - 1)
        sum_r, sum_i = transformed(jnp.where(single, a_r, a_r + b_r), jnp.where(single, a_i, a_i + b_i))
        dif_r, dif_i = transformed(jnp.where(single, -b_i, a_r - b_r), jnp.where(single, b_r, a_i - b_i))
        cosine = along_x(0, two_terms(jnp.concatenate([sum_r, dif_i], axis=1)))
        sine = along_x(1, two_terms(jnp.concatenate([sum_i, dif_r], axis=1)))
        fields = (
            (cosine[:, :grid] - sine[:, :grid], cosine[:, :grid] + sine[:, :grid]),
            (cosine[:, grid:] + sine[:, grid:], cosine[:, grid:] - sine[:, grid:]),
        )
        for c in range(2):
            plus, minus = fields[c]
            for part in range(grid // LANES):
                cut = slice(part * LANES, (part + 1) * LANES)
                place = 2 * i + c
                lines[part, pl.ds(place, half, stride=count), :] = plus[:half, cut]
                lines[part, pl.ds(half * count + place, half, stride=count), :] = minus[1 : half + 1, cut]
        return carry

    lax.fori_loop(0, pairs, one, 0, unroll=2)
    for d in range(slabs):
        if d < slabs // 2:
            start = slab * d
        else:
            start = half + grid - slab * d - slab
        size = slab * count
        for part in range(grid // LANES):
            block = lines[part, start * count : start * count + size, :]
            out_ref[d, :, :, part * LANES : (part + 1) * LANES] = block.astype(BF16).reshape(slab, count, LANES)


def planes_call(flag, data, table_y, table_x, slabs, grid):
    parts, sides, values, pitch, _ = data.shape
    step = min(16, values)
    slab = grid // slabs
    fixed = lambda i, flag_ref: (0, 0)
    return pl.pallas_call(
        functools.partial(plane_kernel, slabs, grid),
        grid_spec=pltpu.PrefetchScalarGridSpec(
            num_scalar_prefetch=1,
            grid=(values // step,),
            in_specs=[
                pl.BlockSpec((parts, sides, step, pitch, LANES), lambda i, flag_ref: (0, 0, i, 0, 0)),
                pl.BlockSpec(table_y[0].shape, fixed),
                pl.BlockSpec(table_y[1].shape, fixed),
                pl.BlockSpec(table_x[0].shape, fixed),
                pl.BlockSpec(table_x[1].shape, fixed),
            ],
            out_specs=pl.BlockSpec((slabs, slab, step, grid), lambda i, flag_ref: (0, 0, i, 0)),
            scratch_shapes=[VMEM((parts, grid * step, LANES), F32)],
        ),
        out_shape=jax.ShapeDtypeStruct((slabs, slab, values, grid), BF16),
        compiler_params=pltpu.CompilerParams(vmem_limit_bytes=56 * 2**20),
        name="planes",
    )(flag, data, *table_y, *table_x)


def volume_kernel(flip_ref, data_ref, restore_ref, zh_ref, zl_ref, out_ref):
    slabs, span, width, grid = data_ref.shape
    for i in range(span):
        block = data_ref[:, i].reshape(slabs * width, grid)
        turned = dot_t(restore_ref[...], block).astype(BF16)
        value = dot(turned, zh_ref[...]) + dot(turned, zl_ref[...])
        out_ref[jnp.where(flip_ref[0] == 1, span - 1 - i, i)] = value


def volume_call(flip, data, restore, table_z):
    slabs, slab, width, grid = data.shape
    span = 4
    steps = slab // span
    fixed = lambda i, flip_ref: (0, 0)
    return pl.pallas_call(
        volume_kernel,
        grid_spec=pltpu.PrefetchScalarGridSpec(
            num_scalar_prefetch=1,
            grid=(steps,),
            in_specs=[
                pl.BlockSpec((slabs, span, width, grid), lambda i, flip_ref: (0, i, 0, 0)),
                pl.BlockSpec(restore.shape, fixed),
                pl.BlockSpec(table_z[0].shape, fixed),
                pl.BlockSpec(table_z[1].shape, fixed),
            ],
            out_specs=pl.BlockSpec(
                (span, grid, grid), lambda i, flip_ref: (jnp.where(flip_ref[0] == 1, steps - 1 - i, i), 0, 0)
            ),
        ),
        out_shape=jax.ShapeDtypeStruct((slab, grid, grid), F32),
        compiler_params=pltpu.CompilerParams(vmem_limit_bytes=48 * 2**20),
        name="volume",
    )(flip, data, restore, *table_z)


def sorted_points(interp_cells, grid):
    dirs = interp_cells.shape[0]
    points = dirs * grid
    base = interp_cells[:, 0, :].T.reshape(-1)
    row = (base // grid + 1) & (grid - 1)
    key = row * points + jnp.arange(points, dtype=jnp.int32)
    key = lax.sort(key, is_stable=False)
    rows = jnp.arange(grid, dtype=jnp.int32)
    count = jnp.sum((row[None, :] == rows[:, None]).astype(jnp.int32), axis=1)
    first = jnp.cumsum(count) - count
    chunks = jnp.maximum((count + (CHUNK - 1)) // CHUNK, 1)
    ends = jnp.cumsum(chunks)
    most = grid + points // CHUNK + UNROLL + 1
    number = jnp.arange(most, dtype=jnp.int32)
    chunk_row = jnp.minimum(jnp.sum((ends[None, :] <= number[:, None]).astype(jnp.int32), axis=1), grid - 1)
    mine = (rows[None, :] == chunk_row[:, None]).astype(jnp.int32)
    shift = first - (ends - chunks) * CHUNK
    chunk_start = jnp.sum(mine * shift[None, :], axis=1) + number * CHUNK
    row_end = jnp.sum(mine * (first + count)[None, :], axis=1)
    used = number < ends[-1]
    chunk_size = jnp.where(used, jnp.clip(row_end - chunk_start, 0, CHUNK), 0)
    chunk_start = jnp.where(used, chunk_start, points)
    turns = ((ends[-1] + (UNROLL - 1)) // UNROLL).reshape(1)
    point = jnp.concatenate([key & (points - 1), jnp.zeros((CHUNK,), jnp.int32)])
    return turns, chunk_row, chunk_start, chunk_size, point


def arrange_kernel(rows_ref, eye_ref, order_ref, kept_ref, sent_ref, *lines):
    dirs, count, _, grid = rows_ref.shape
    blocks = LANES // count
    length = grid // blocks
    lane = lax.broadcasted_iota(jnp.int32, (length, LANES), 1)

    def step(m, carry):
        block = rows_ref[pl.ds(blocks * m, blocks)].reshape(2 * LANES, grid)
        turned = dot(dot_t(eye_ref[...], block).astype(BF16), order_ref[...])
        for side in range(2):
            tile = [turned[q * length : (q + 1) * length, side * LANES : (side + 1) * LANES] for q in range(blocks)]
            for i in range(blocks):
                out = tile[i]
                for q in range(blocks):
                    if q != i:
                        moved = pltpu.roll(tile[q], (q - i) * count % LANES, 1)
                        out = jnp.where((lane >= q * count) & (lane < (q + 1) * count), moved, out)
                lines[side][pl.ds(blocks * m + i, length, stride=dirs), :] = out
        return carry

    lax.fori_loop(0, dirs // blocks, step, 0, unroll=2)
    kept_ref[...] = lines[0][...].astype(BF16).reshape(kept_ref.shape)
    sent_ref[...] = lines[1][...].astype(BF16).reshape(sent_ref.shape)


def arrange_call(rows, eye, order, steps):
    dirs, count, _, grid = rows.shape
    length = grid // (LANES // count)
    vmem = pl.BlockSpec(memory_space=VMEM)
    shape = jax.ShapeDtypeStruct((length // steps, steps * dirs, LANES), BF16)
    return pl.pallas_call(
        arrange_kernel,
        out_shape=(shape, shape),
        in_specs=[vmem] * 3,
        out_specs=(vmem, vmem),
        scratch_shapes=[VMEM((length * dirs, LANES), F32)] * 2,
        compiler_params=pltpu.CompilerParams(vmem_limit_bytes=48 * 2**20),
        name="arrange",
    )(rows, eye, order)


def row_orders(slab):
    half = slab // 2
    blocks = LANES // slab
    orders = []
    for kept, sent in (
        (range(1, half + 1), [*range(half + 1, slab), 0]),
        (range(half - 1, -1, -1), range(slab - 1, half - 1, -1)),
    ):
        order = np.zeros((2 * LANES, 2 * LANES), np.float32)
        for side, rows in enumerate((kept, sent)):
            for k in range(blocks):
                for i, row in enumerate(rows):
                    for r in range(2):
                        order[(k * slab + row) * 2 + r, side * LANES + k * slab + 2 * i + r] = 1.0
        orders.append(order.astype(jnp.bfloat16))
    return orders


def paired_rows(rows, other, eye, slabs, steps):
    own = lax.axis_index("vol")
    rows = jnp.concatenate([jnp.where(own <= slabs // 2, other, rows[:, :1]), rows[:, 1:]], axis=1)
    lower, upper = row_orders(rows.shape[1])
    order = jnp.where(own < slabs // 2, jnp.asarray(lower), jnp.asarray(upper))
    kept, sent = arrange_call(rows, eye, order, steps)
    arrived = lax.ppermute(sent, "vol", [(i, slabs - 1 - i) for i in range(slabs)])
    return kept, arrived


def shards(images, projections, assignment, interp_cells, interp_weights):
    class_count = lax.axis_size("cls")
    slab_count = lax.axis_size("vol")
    local_count, grid = images.shape[0], images.shape[1]
    dirs = projections.shape[1]
    slab = grid // slab_count
    width = 2 * slab
    halves = LANES // width
    capacity = 2 * local_count // class_count
    steps = 16 // capacity
    groups = grid // (halves * steps)

    eye = jnp.asarray(np.eye(grid), BF16)
    order = jnp.asarray(lane_order(grid, slab_count))
    outgoing = route_call(images, assignment, eye, order, class_count, slab_count, width, capacity)
    first = [(0, slab_count // 2)] + [(i, i - 1) for i in range(1, slab_count // 2 + 1)]
    other = lax.ppermute(projections[0, :, :1], "vol", first)
    outgoing, projections, other = lax.optimization_barrier((outgoing, projections, other))
    arrived = lax.all_to_all(outgoing, ("cls", "vol"), split_axis=0, concat_axis=0, tiled=True)

    kept, joined = paired_rows(projections[0], other, eye, slab_count, steps)
    corner_y = (interp_cells[:, 0:1, :] & (grid - 1)).astype(F32)
    weights = jnp.concatenate([interp_weights, corner_y, jnp.zeros((dirs, 3, grid), F32)], axis=1)
    weights = weights.reshape(dirs, 8, halves, groups, steps)
    weights = jnp.transpose(weights, (3, 4, 0, 2, 1)).reshape(groups, steps * dirs, 8 * halves)
    weights = jnp.pad(weights, ((0, 0), (0, 0), (0, LANES - 8 * halves)))
    plan = sorted_points(interp_cells, grid)
    table_y, table_x, table_z, restore = tables(grid, slab_count)

    arrived, kept, joined, weights, plan = lax.optimization_barrier((arrived, kept, joined, weights, plan))
    partial_value = scores_call(arrived, kept, joined, capacity, dirs, slab)
    copies = jnp.broadcast_to(partial_value[None], (slab_count,) + partial_value.shape)
    parts = lax.all_to_all(copies, "vol", split_axis=0, concat_axis=0, tiled=True)
    plane = scatter_call(plan, parts, arrived, weights, capacity, width, grid)
    plane = plane.reshape(grid // LANES, 2, slab, grid + PAD, LANES)
    own = lax.axis_index("vol")
    single = (own == slab_count // 2).astype(jnp.int32).reshape(1)
    flip = (own >= slab_count // 2).astype(jnp.int32).reshape(1)
    sent = planes_call(single, plane, table_y, table_x, slab_count, grid)
    received = lax.all_to_all(sent, "vol", split_axis=0, concat_axis=0, tiled=True)
    return volume_call(flip, received, restore, table_z)[None]


def solution(mesh):
    in_specs = (
        P(("cls", "vol"), None, None, None),
        P("cls", None, "vol", None, None),
        P(("cls", "vol"), None),
        P(),
        P(),
    )
    out_specs = P("cls", "vol", None, None)
    return jax.shard_map(shards, mesh=mesh, in_specs=in_specs, out_specs=out_specs, check_vma=False)
```

profile of v0, /device:TPU:0, one launch (start us, length us, event | category | flops | bytes accessed | tf_op | source)
XLA Modules:
  0.0 319.5 jit_solution(7902123269062484680)
XLA Ops:
  0.0 1.0 slice_bitcast_fusion
  1.0 4.9 %collective-permute-start = (bf16[128,1,2,256]{3,2,1,0:T(2,128)(2,1)S(1)}, bf16[128,1,2,256]{3,2,1,0:T(2,128)(2,1)S(1)}, u32[]{:S(2)}, u32[]{:S(2)}) collective-permute-start(bf16[128,1,2,256]{3,2,1,0:T(2,128)(2,1)S(1)} %slice_bitcast_fusion), channel_id=1, source_target_pairs={{0,4},{1,0},{2,1},{3,2},{4,3},{8,12},{9,8},{10,9},{11,10},{12,11},... | collective-permute-start | bytes 393224 | tf_op jit(solution)/shard_map/ppermute | solution.py:566
  5.9 0.7 copy.28.classes_ref
  6.6 1.6 copy-done
  8.2 1.0 copy-done.1
  9.3 0.9 copy-done.2
  10.2 7.0 %route.1 = bf16[32,32,16,128]{3,2,1,0:T(8,128)(2,1)} custom-call(s32[8,1]{1,0:T(8,128)S(1)} %copy.28.classes_ref, bf16[8,256,2,256]{3,2,1,0:T(2,128)(2,1)S(1)} %copy-done, bf16[256,256]{1,0:T(8,128)(2,1)S(1)} %copy-done.2, bf16[512,512]{1,0:T(8,128)(2,1)S(1)} %copy-done.1), custom_call_target="tpu_custom_call" | custom-call | tf_op jit(solution)/shard_map/route/pallas_call | solution.py:124
  17.2 4.4 %all-to-all-start = ((bf16[32,32,16,128]{3,2,1,0:T(8,128)(2,1)}), bf16[32,32,16,128]{3,2,1,0:T(8,128)(2,1)}, u32[]{:S(2)}, u32[]{:S(2)}) async-start(bf16[32,32,16,128]{3,2,1,0:T(8,128)(2,1)} %route.1), calls=%async_computation | async-start | bytes 8388608 | tf_op jit(solution)/shard_map/all_to_all | solution.py:568
  21.6 0.1 copy.38
  21.7 0.1 iota_add_fusion
  21.9 3.7 %convert_reduce_fusion = s32[256]{0:T(256)S(1)} fusion(s32[32768]{0:T(1024)S(1)} %get-tuple-element.36), kind=kLoop, calls=%fused_computation | loop fusion | flops 25165568 | bytes 132096 | tf_op jit(solution)/shard_map/reduce_sum | solution.py:462
  25.6 0.3 reduce-window.16
  25.9 0.1 slice.35
  26.0 0.3 reduce-window.24
  26.3 0.1 slice.38
  26.5 0.1 slice_reduce_fusion
  26.6 4.9 %slice.41 = bf16[128,31,2,256]{3,2,1,0:T(2,128)(2,1)S(1)} slice(bf16[128,32,2,256]{3,2,1,0:T(2,128)(2,1)} %bitcast.32), slice={[0:128], [1:32], [0:2], [0:256]} | slice | bytes 8126464 | tf_op jit(solution)/shard_map/slice | solution.py:542
  31.6 1.0 broadcast_select_fusion
  32.6 0.0 copy-start.3
  32.7 7.6 %pad_maximum_fusion.rows_ref = bf16[128,32,2,256]{3,2,1,0:T(2,128)(2,1)} fusion(bf16[128,31,2,256]{3,2,1,0:T(2,128)(2,1)S(1)} %slice.41, bf16[128,1,2,256]{3,2,1,0:T(2,128)(2,1)S(1)} %broadcast_select_fusion), kind=kLoop, calls=%fused_computation.2 | loop fusion | flops 2097152 | bytes 8388608 | tf_op jit(solution)/shard_map/concatenate | solution.py:542
  40.3 21.3 %arrange.1 = (bf16[16,512,128]{2,1,0:T(8,128)(2,1)S(1)}, bf16[16,512,128]{2,1,0:T(8,128)(2,1)}) custom-call(bf16[128,32,2,256]{3,2,1,0:T(2,128)(2,1)} %pad_maximum_fusion.rows_ref, bf16[256,256]{1,0:T(8,128)(2,1)S(1)} %copy-done.3, bf16[256,256]{1,0:T(8,128)(2,1)S(1)} %broadcast_select_fusion.1.order_ref), custom_call_target="tpu_custom_call" | custom-call | tf_op jit(solution)/shard_map/arrange/pallas_call | solution.py:511
  61.5 2.3 collective-permute-start.1
  63.9 0.1 multiply_subtract_fusion
  64.0 0.6 slice.37
  65.1 7.3 %sort.7 = s32[32768]{0:T(1024)S(1)} sort(s32[32768]{0:T(1024)S(1)} %get-tuple-element.35), dimensions={0}, to_apply=%region_8.9 | sort | flops 491520 | bytes 262144 | tf_op jit(solution)/shard_map/sort | solution.py:460
  72.4 0.7 concatenate.11.point_ref
  73.1 0.3 copy.31
  73.4 0.1 pad.8.clone
  73.5 0.1 and_convert_fusion
  73.6 0.2 maximum_maximum_fusion
  73.8 1.3 copy.32
  75.1 1.6 reshape.157
  76.8 4.6 %copy.33 = f32[32,512,16]{2,1,0:T(8,128)} copy(f32[32,512,16]{1,2,0:T(8,128)S(1)} %reshape.157) | data formatting | bytes 2097152 | tf_op jit(solution)/shard_map/reshape | solution.py:574
  81.4 7.6 %pad.5.weights_ref = f32[32,512,128]{2,1,0:T(8,128)} pad(f32[32,512,16]{2,1,0:T(8,128)} %copy.33, f32[]{:T(128)} %constant.84.clone.1), padding=0_0x0_0x0_112 | pad | bytes 9437188 | tf_op jit(solution)/shard_map/jit(_pad)/pad | solution.py:575
  89.0 0.2 convert_reduce_fusion.1
  89.2 0.3 select_reduce_fusion
  89.5 1.2 clamp_select_fusion
  90.7 38.4 %collective-permute-done.1.joined_ref = bf16[16,512,128]{2,1,0:T(8,128)(2,1)} collective-permute-done((bf16[16,512,128]{2,1,0:T(8,128)(2,1)}, bf16[16,512,128]{2,1,0:T(8,128)(2,1)}, u32[]{:S(2)}, u32[]{:S(2)}) %collective-permute-start.1) | collective-permute-done | bytes 2097184 | tf_op jit(solution)/shard_map/ppermute | solution.py:546
  129.1 7.3 %scores.1 = f32[128,128]{1,0:T(8,128)S(1)} custom-call(bf16[32,32,16,128]{3,2,1,0:T(8,128)(2,1)} %all-to-all-done.images_ref, bf16[16,512,128]{2,1,0:T(8,128)(2,1)S(1)} %get-tuple-element.30.kept_ref, bf16[16,512,128]{2,1,0:T(8,128)(2,1)} %collective-permute-done.1.joined_ref), custom_call_target="tpu_custom_call" | custom-call | tf_op jit(solution)/shard_map/scores/pallas_call | solution.py:171
  136.5 0.8 broadcast_in_dim.13
  137.3 3.5 %all-to-all-start.1 = ((f32[8,128,128]{2,1,0:T(8,128)}), f32[8,128,128]{2,1,0:T(8,128)S(1)}, u32[]{:S(2)}, u32[]{:S(2)}) async-start(f32[8,128,128]{2,1,0:T(8,128)} %broadcast_in_dim.13), calls=%async_computation.1 | async-start | bytes 1048576 | tf_op jit(solution)/shard_map/all_to_all | solution.py:582
  140.8 9.7 %all-to-all-done.1.parts_ref = f32[8,128,128]{2,1,0:T(8,128)S(1)} async-done(((f32[8,128,128]{2,1,0:T(8,128)}), f32[8,128,128]{2,1,0:T(8,128)S(1)}, u32[]{:S(2)}, u32[]{:S(2)}) %all-to-all-start.1) | async-done | bytes 524320 | tf_op jit(solution)/shard_map/all_to_all | solution.py:582
  150.5 0.8 copy-done.7
  151.3 80.9 %scatter.1 = f32[2,16896,128]{2,1,0:T(8,128)} custom-call(s32[1]{0:T(128)} %bitcast.16.turns_ref, s32[521]{0:T(1024)} %copy-done.11, s32[521]{0:T(1024)} %get-tuple-element.26.chunk_start_ref, s32[521]{0:T(1024)} %get-tuple-element.27.chunk_size_ref, s32[32896]{0:T(1024)} %concatenate.11.point_ref, f32[8,128,128]{2,1,0:T(8,128)} %copy-done.7, ...), custom_call_target="tpu_custom_call" | custom-call | tf_op jit(solution)/shard_map/scatter/pallas_call | solution.py:309
  232.2 23.0 %planes.1 = bf16[8,32,32,256]{3,2,1,0:T(8,128)(2,1)} custom-call(s32[1]{0:T(128)} %bitcast.1.flag_ref, f32[2,2,32,264,128]{4,3,2,1,0:T(8,128)} %bitcast.31, bf16[256,256]{1,0:T(8,128)(2,1)} %constant.99.clone.yh_ref, bf16[256,256]{1,0:T(8,128)(2,1)} %constant.100.clone.yl_ref, bf16[272,256]{1,0:T(8,128)(2,1)} %constant.101.clone.xh_ref, ...), custom_call_target="tpu_custom_call" | custom-call | tf_op jit(solution)/shard_map/planes/pallas_call | solution.py:398
  255.2 4.7 %all-to-all-start.2 = ((bf16[8,32,32,256]{3,2,1,0:T(8,128)(2,1)}), bf16[8,32,32,256]{3,2,1,0:T(8,128)(2,1)}, u32[]{:S(2)}, u32[]{:S(2)}) async-start(bf16[8,32,32,256]{3,2,1,0:T(8,128)(2,1)} %planes.1), calls=%async_computation.2 | async-start | bytes 8388608 | tf_op jit(solution)/shard_map/all_to_all | solution.py:589
  259.9 49.1 %all-to-all-done.2.data_ref = bf16[8,32,32,256]{3,2,1,0:T(8,128)(2,1)} async-done(((bf16[8,32,32,256]{3,2,1,0:T(8,128)(2,1)}), bf16[8,32,32,256]{3,2,1,0:T(8,128)(2,1)}, u32[]{:S(2)}, u32[]{:S(2)}) %all-to-all-start.2) | async-done | bytes 4194336 | tf_op jit(solution)/shard_map/all_to_all | solution.py:589
  309.0 10.4 %volume.1 = f32[32,256,256]{2,1,0:T(8,128)} custom-call(s32[1]{0:T(128)} %bitcast.flip_ref, bf16[8,32,32,256]{3,2,1,0:T(8,128)(2,1)} %all-to-all-done.2.data_ref, bf16[256,256]{1,0:T(8,128)(2,1)S(1)} %copy-done.4, bf16[256,256]{1,0:T(8,128)(2,1)S(1)} %copy-done.5, bf16[256,256]{1,0:T(8,128)(2,1)S(1)} %copy-done.6), custom_call_target="tpu_custom_call" | custom-call | tf_op jit(solution)/shard_map/volume/pallas_call | solution.py:433
  (30 shorter events, 0.2 us)
Async XLA Ops:
  1.0 16.2 %collective-permute-start = (bf16[128,1,2,256]{3,2,1,0:T(2,128)(2,1)S(1)}, bf16[128,1,2,256]{3,2,1,0:T(2,128)(2,1)S(1)}, u32[]{:S(2)}, u32[]{:S(2)}) collective-permute-start(bf16[128,1,2,256]{3,2,1,0:T(2,128)(2,1)S(1)} %slice_bitcast_fusion), channel_id=1, source_target_pairs={{0,4},{1,0},{2,1},{3,2},{4,3},{8,12},{9,8},{10,9},{11,10},{12,11},... | collective-permute-start | bytes 393224 | tf_op jit(solution)/shard_map/ppermute | solution.py:566
  6.6 1.6 copy-start
  8.2 1.0 copy-start.1
  9.2 0.9 copy-start.2
  17.2 4.4 %slice-start = ((s32[128,4,256]{2,1,0:T(4,128)}), s32[128,1,256]{2,1,0:T(1,128)S(1)}, s32[]{:S(2)}) async-start(s32[128,4,256]{2,1,0:T(4,128)} %param.19), calls=%async_computation.3 | async-start | bytes 262144 | tf_op jit(solution)/shard_map/slice | solution.py:571
  17.2 9.4 %copy-start.9 = (bf16[256,256]{1,0:T(8,128)(2,1)S(1)}, bf16[256,256]{1,0:T(8,128)(2,1)}, u32[]{:S(2)}) copy-start(bf16[256,256]{1,0:T(8,128)(2,1)} %constant.97.clone) | copy-start | bytes 393220
  17.2 9.4 %copy-start.10 = (bf16[256,256]{1,0:T(8,128)(2,1)S(1)}, bf16[256,256]{1,0:T(8,128)(2,1)}, u32[]{:S(2)}) copy-start(bf16[256,256]{1,0:T(8,128)(2,1)} %constant.98.clone) | copy-start | bytes 393220
  17.2 111.9 %all-to-all-start = ((bf16[32,32,16,128]{3,2,1,0:T(8,128)(2,1)}), bf16[32,32,16,128]{3,2,1,0:T(8,128)(2,1)}, u32[]{:S(2)}, u32[]{:S(2)}) async-start(bf16[32,32,16,128]{3,2,1,0:T(8,128)(2,1)} %route.1), calls=%async_computation | async-start | bytes 8388608 | tf_op jit(solution)/shard_map/all_to_all | solution.py:568
  32.6 7.6 %copy-start.3 = (bf16[256,256]{1,0:T(8,128)(2,1)S(1)}, bf16[256,256]{1,0:T(8,128)(2,1)}, u32[]{:S(2)}) copy-start(bf16[256,256]{1,0:T(8,128)(2,1)} %constant.95.clone.eye_ref) | copy-start | bytes 393220
  40.2 32.9 %copy-start.8 = (f32[128,4,256]{2,1,0:T(4,128)S(1)}, f32[128,4,256]{2,1,0:T(4,128)}, u32[]{:S(2)}) copy-start(f32[128,4,256]{2,1,0:T(4,128)} %param.20) | copy-start | bytes 1572868
  61.5 67.6 %collective-permute-start.1 = (bf16[16,512,128]{2,1,0:T(8,128)(2,1)}, bf16[16,512,128]{2,1,0:T(8,128)(2,1)}, u32[]{:S(2)}, u32[]{:S(2)}) collective-permute-start(bf16[16,512,128]{2,1,0:T(8,128)(2,1)} %get-tuple-element.23), channel_id=1, source_target_pairs={{0,7},{1,6},{2,5},{3,4},{4,3},{5,2},{6,1},{7,0},{8,15},{9,14},{10,... | collective-permute-start | bytes 6291464 | tf_op jit(solution)/shard_map/ppermute | solution.py:546
  89.2 47.3 %copy-start.11 = (s32[521]{0:T(1024)}, s32[521]{0:T(1024)S(1)}, u32[]{:S(2)}) copy-start(s32[521]{0:T(1024)S(1)} %broadcast_minimum_fusion.chunk_row_ref) | copy-start | bytes 6256
  137.3 13.2 %all-to-all-start.1 = ((f32[8,128,128]{2,1,0:T(8,128)}), f32[8,128,128]{2,1,0:T(8,128)S(1)}, u32[]{:S(2)}, u32[]{:S(2)}) async-start(f32[8,128,128]{2,1,0:T(8,128)} %broadcast_in_dim.13), calls=%async_computation.1 | async-start | bytes 1048576 | tf_op jit(solution)/shard_map/all_to_all | solution.py:582
  150.5 0.8 copy-start.7
  255.2 53.8 %copy-start.4 = (bf16[256,256]{1,0:T(8,128)(2,1)S(1)}, bf16[256,256]{1,0:T(8,128)(2,1)}, u32[]{:S(2)}) copy-start(bf16[256,256]{1,0:T(8,128)(2,1)} %constant.103.clone.restore_ref) | copy-start | bytes 393220
  255.2 53.8 %copy-start.5 = (bf16[256,256]{1,0:T(8,128)(2,1)S(1)}, bf16[256,256]{1,0:T(8,128)(2,1)}, u32[]{:S(2)}) copy-start(bf16[256,256]{1,0:T(8,128)(2,1)} %constant.104.clone.zh_ref) | copy-start | bytes 393220
  255.2 53.8 %copy-start.6 = (bf16[256,256]{1,0:T(8,128)(2,1)S(1)}, bf16[256,256]{1,0:T(8,128)(2,1)}, u32[]{:S(2)}) copy-start(bf16[256,256]{1,0:T(8,128)(2,1)} %constant.105.clone.zl_ref) | copy-start | bytes 393220
  255.2 53.8 %all-to-all-start.2 = ((bf16[8,32,32,256]{3,2,1,0:T(8,128)(2,1)}), bf16[8,32,32,256]{3,2,1,0:T(8,128)(2,1)}, u32[]{:S(2)}, u32[]{:S(2)}) async-start(bf16[8,32,32,256]{3,2,1,0:T(8,128)(2,1)} %planes.1), calls=%async_computation.2 | async-start | bytes 8388608 | tf_op jit(solution)/shard_map/all_to_all | solution.py:589
where the time goes:
time: 324 us; the launch traced here: 319 us
  Pallas kernels  150 us (46%)
  waiting for transfers between devices  97.2 us (30%)
  local copies, waits for them, and re-layouts  29 us (9%)
  other arithmetic  22.6 us (7%)
  starting transfers between devices  19.8 us (6%)
    pallas_call x1, Pallas kernels, scatter_call(): pl.pallas_call(functools.partial(scatter_kernel, cap, width, grid), out_s...  80.9 us
    all_to_all x1, waiting for transfers between devices, shards(): lax.all_to_all(sent, 'vol', split_axis=0, concat_axis=0, tiled=True)  49.1 us
    ppermute x1, waiting for transfers between devices, paired_rows(): lax.ppermute(sent, 'vol', [(i, slabs - 1 - i) for i in range(slabs)])  38.4 us
    pallas_call x1, Pallas kernels, planes_call(): pl.pallas_call(functools.partial(plane_kernel, slabs, grid), grid_spec=pl...  23 us
    pallas_call x1, Pallas kernels, arrange_call(): pl.pallas_call(arrange_kernel, out_shape=(shape, shape), in_specs=[vmem]...  21.3 us
    pallas_call x1, Pallas kernels, volume_call(): pl.pallas_call(volume_kernel, grid_spec=pltpu.PrefetchScalarGridSpec(num_...  10.4 us
    all_to_all x1, waiting for transfers between devices, shards(): lax.all_to_all(copies, 'vol', split_axis=0, concat_axis=0, tiled=True)  9.68 us
    pad x1, local copies, waits for them, and re-layouts, shards(): weights = jnp.pad(weights, ((0, 0), (0, 0), (0, LANES - 8 * halves)))  7.6 us
  transfers between devices with their start and end apart: 5, of which 3 were waited for; matrix products, arithmetic and copies ran while one was open for 14% of the time, Pallas kernels for 9%

commit v1 on v0

--- a/solution.py
+++ b/solution.py
@@ -16,6 +16,7 @@
 CHUNK = 128
 PAD = 8
 UNROLL = 8
+STEP = 16
 VMEM = pltpu.VMEM
 
 
@@ -65,7 +66,14 @@
     table_z = np.stack([for_sum, for_difference], axis=1).reshape(grid, grid) * scale
     order = np.concatenate([np.arange(half), [half], np.arange(grid - 1, half, -1)])
     restore = (order[None, :] == index[:, None]).astype(jnp.bfloat16)
-    return split_table(table_y), split_table(table_x), split_table(table_z), restore
+    parts = max(1, grid // slabs // STEP)
+    table_z = table_z.reshape(slabs, parts, -1, grid).transpose(1, 0, 2, 3).reshape(grid, grid)
+    high, low = split_table(table_y)
+    table_y = np.concatenate([high, high, low], axis=0)
+    high, low = split_table(table_x)
+    table_x = np.concatenate([high, high, low], axis=1)
+    table_z = np.concatenate(split_table(table_z), axis=0)
+    return table_y, table_x, table_z, restore
 
 
 def lane_order(grid, slabs):
@@ -183,10 +191,7 @@
     cap,
     width,
     grid,
-    turns_ref,
-    chunk_row_ref,
-    chunk_start_ref,
-    chunk_size_ref,
+    first_ref,
     point_ref,
     parts_ref,
     images_ref,
@@ -244,8 +249,10 @@
     one = jnp.ones((CHUNK, grid), BF16)
     none = jnp.zeros((CHUNK, grid), BF16)
 
-    def fetch(c, buffer):
-        start = chunk_start_ref[c]
+    lane_1 = lax.broadcasted_iota(jnp.int32, (1, CHUNK), 1)
+    points = values.shape[0]
+
+    def fetch(start, buffer):
         for i in range(0, CHUNK, 8):
             block = jnp.broadcast_to(values[pl.ds(point_ref[start + i], 1), :], (8, LANES))
             for j in range(1, 8):
@@ -253,51 +260,73 @@
                 block = jnp.where(line_8 == j, line, block)
             buffer[i : i + 8, :] = block
 
-    def put(x, plane):
+    def put(row, plane):
+        x = (row + (grid - 1)) & (grid - 1)
         for side in range(grid // LANES):
             out_ref[side, pl.ds(x, width, stride=grid + PAD), :] = plane[:, side * LANES : (side + 1) * LANES]
 
-    def work(c, buffer):
-        row = chunk_row_ref[c]
-        before = chunk_row_ref[jnp.maximum(c - 1, 0)]
+    def following(start, row):
+        second, third = first_ref[row + 1], first_ref[row + 2]
+        end = jnp.minimum(start + CHUNK, third)
+        moved = row + jnp.where(end >= second, 1, 0) + jnp.where(end >= third, 1, 0)
+        return end, jnp.minimum(moved, grid - 1), end - start, jnp.clip(second - start, 0, end - start)
+
+    def work(row, before, size, size_0, buffer):
         data = buffer[...]
         y = jnp.broadcast_to(data[:, HALF + 4 : HALF + 5], (CHUNK, LANES))
-        y = jnp.where(place < chunk_size_ref[c], y, -1.0).astype(BF16)
+        y = jnp.where(place < size, y, -1.0).astype(BF16)
         y = jnp.concatenate([y] * (grid // LANES), axis=1)
         hot = jnp.concatenate([jnp.where(at_y == y, one, none), jnp.where(at_next == y, one, none)], axis=0)
         turned = data.T
         mean = turned[:width]
-        weight = [jnp.broadcast_to(turned[HALF + j : HALF + j + 1], (width, CHUNK)) for j in range(4)]
+        weight = [turned[HALF + j : HALF + j + 1] for j in range(4)]
+        here = [jnp.where(lane_1 < size_0, w, 0.0) for w in weight]
+        there = [w - h for w, h in zip(weight, here)]
+        by_row = (
+            (here[0], here[2]),
+            (here[1] + there[0], here[3] + there[2]),
+            (there[1], there[3]),
+        )
         operand = jnp.concatenate(
             [
-                jnp.concatenate([mean * weight[0], mean * weight[2]], axis=1),
-                jnp.concatenate([mean * weight[1], mean * weight[3]], axis=1),
+                jnp.concatenate([mean * jnp.broadcast_to(w, (width, CHUNK)) for w in pair], axis=1)
+                for pair in by_row
             ],
             axis=0,
         )
         high, low = two_terms(operand)
         result = dot(jnp.concatenate([high, low], axis=0), hot)
-        result = result[: 2 * width] + result[2 * width :]
-        same = row == before
-        old_low, old_high = sums[:width], sums[width:]
-        put((before + (grid - 1)) & (grid - 1), old_low)
-        sums[:width] = result[:width] + jnp.where(same, old_low, old_high)
-        sums[width:] = result[width:] + jnp.where(same, old_high, 0.0)
+        result = result[: 3 * width] + result[3 * width :]
+        old = [sums[i * width : (i + 1) * width] for i in range(3)]
+        put(jnp.minimum(before + 1, grid - 1), old[1])
+        put(before, old[0])
+        stay, by_one = row == before, row == before + 1
+        kept = (
+            jnp.where(stay, old[0], jnp.where(by_one, old[1], old[2])),
+            jnp.where(stay, old[1], jnp.where(by_one, old[2], 0.0)),
+            jnp.where(stay, old[2], 0.0),
+        )
+        for i in range(3):
+            sums[i * width : (i + 1) * width] = result[i * width : (i + 1) * width] + kept[i]
 
     fetch(0, buffers[0])
 
-    def several(m, carry):
+    def several(state):
+        start, row, before = state
         for i in range(UNROLL):
-            fetch(UNROLL * m + i + 1, buffers[(i + 1) % UNROLL])
-            work(UNROLL * m + i, buffers[i])
-        return carry
-
-    lax.fori_loop(0, turns_ref[0], several, 0)
-    put(grid - 2, sums[:width])
+            end, moved, size, size_0 = following(start, row)
+            fetch(end, buffers[(i + 1) % UNROLL])
+            work(row, before, size, size_0, buffers[i])
+            start, row, before = end, moved, row
+        return start, row, before
+
+    zero = jnp.int32(0)
+    lax.while_loop(lambda state: (state[0] < points) | (state[2] < grid - 1), several, (zero, zero, zero))
+    put(grid - 1, sums[:width])
     for side in range(grid // LANES):
         wrapped = pl.ds(grid - 1, width, stride=grid + PAD)
         cut = slice(side * LANES, (side + 1) * LANES)
-        out_ref[side, wrapped, :] = out_ref[side, wrapped, :] + sums[width:, cut]
+        out_ref[side, wrapped, :] = out_ref[side, wrapped, :] + sums[width : 2 * width, cut]
 
 
 def scatter_call(plan, parts, images, weights, cap, width, grid):
@@ -309,11 +338,11 @@
     return pl.pallas_call(
         functools.partial(scatter_kernel, cap, width, grid),
         out_shape=jax.ShapeDtypeStruct((grid // LANES, width * (grid + PAD), LANES), F32),
-        in_specs=[smem] * 5 + [vmem] * 3,
+        in_specs=[smem] * 2 + [vmem] * 3,
         out_specs=vmem,
         scratch_shapes=[
             VMEM((points, LANES), F32),
-            VMEM((2 * width, grid), F32),
+            VMEM((3 * width, grid), F32),
             VMEM((weights.shape[1], sources * rows16), BF16),
         ]
         + [VMEM((CHUNK, LANES), F32)] * UNROLL,
@@ -322,18 +351,18 @@
     )(*plan, parts, images, weights)
 
 
-def plane_kernel(slabs, grid, flag_ref, data_ref, yh_ref, yl_ref, xh_ref, xl_ref, out_ref, lines):
+def plane_kernel(slabs, grid, final, flag_ref, data_ref, y_ref, x_ref, out_ref, lines):
     pairs = data_ref.shape[2] // 2
     half = grid // 2
     rows = half + 8
     slab = grid // slabs
     count = 2 * pairs
     lane = lax.broadcasted_iota(jnp.int32, (grid, half), 1)
-    last = (pl.program_id(0) == pl.num_programs(0) - 1) & (flag_ref[0] == 1)
+    last = (flag_ref[0] == 1) & final
 
     def along_y(plane):
         high, low = two_terms(plane)
-        both = dot(high, yh_ref[...]) + dot(low, yh_ref[...]) + dot(high, yl_ref[...])
+        both = dot(jnp.concatenate([high, low, high], axis=1), y_ref[...])
         return both[:, :half], both[:, half:]
 
     def transformed(real, imag):
@@ -348,8 +377,7 @@
     def along_x(table, operand):
         high, low = operand
         start = table * rows
-        upper, lower = xh_ref[start : start + rows], xl_ref[start : start + rows]
-        return dot(upper, high) + dot(upper, low) + dot(lower, high)
+        return dot(x_ref[start : start + rows], jnp.concatenate([high, low, high], axis=0))
 
     def one(i, carry):
         planes = [
@@ -390,43 +418,43 @@
             out_ref[d, :, :, part * LANES : (part + 1) * LANES] = block.astype(BF16).reshape(slab, count, LANES)
 
 
-def planes_call(flag, data, table_y, table_x, slabs, grid):
+def planes_call(flag, data, table_y, table_x, slabs, grid, part):
     parts, sides, values, pitch, _ = data.shape
-    step = min(16, values)
+    step = min(STEP, values)
     slab = grid // slabs
+    final = part == values // step - 1
     fixed = lambda i, flag_ref: (0, 0)
     return pl.pallas_call(
-        functools.partial(plane_kernel, slabs, grid),
+        functools.partial(plane_kernel, slabs, grid, final),
         grid_spec=pltpu.PrefetchScalarGridSpec(
             num_scalar_prefetch=1,
-            grid=(values // step,),
+            grid=(1,),
             in_specs=[
-                pl.BlockSpec((parts, sides, step, pitch, LANES), lambda i, flag_ref: (0, 0, i, 0, 0)),
-                pl.BlockSpec(table_y[0].shape, fixed),
-                pl.BlockSpec(table_y[1].shape, fixed),
-                pl.BlockSpec(table_x[0].shape, fixed),
-                pl.BlockSpec(table_x[1].shape, fixed),
+                pl.BlockSpec((parts, sides, step, pitch, LANES), lambda i, flag_ref: (0, 0, part, 0, 0)),
+                pl.BlockSpec(table_y.shape, fixed),
+                pl.BlockSpec(table_x.shape, fixed),
             ],
-            out_specs=pl.BlockSpec((slabs, slab, step, grid), lambda i, flag_ref: (0, 0, i, 0)),
+            out_specs=pl.BlockSpec((slabs, slab, step, grid), lambda i, flag_ref: (0, 0, 0, 0)),
             scratch_shapes=[VMEM((parts, grid * step, LANES), F32)],
         ),
-        out_shape=jax.ShapeDtypeStruct((slabs, slab, values, grid), BF16),
+        out_shape=jax.ShapeDtypeStruct((slabs, slab, step, grid), BF16),
         compiler_params=pltpu.CompilerParams(vmem_limit_bytes=56 * 2**20),
         name="planes",
-    )(flag, data, *table_y, *table_x)
-
-
-def volume_kernel(flip_ref, data_ref, restore_ref, zh_ref, zl_ref, out_ref):
-    slabs, span, width, grid = data_ref.shape
+    )(flag, data, table_y, table_x)
+
+
+def volume_kernel(flip_ref, restore_ref, z_ref, *refs):
+    out_ref = refs[-1]
+    slabs, span, width, grid = refs[0].shape
     for i in range(span):
-        block = data_ref[:, i].reshape(slabs * width, grid)
+        block = jnp.concatenate([ref[:, i].reshape(slabs * width, grid) for ref in refs[:-1]], axis=0)
         turned = dot_t(restore_ref[...], block).astype(BF16)
-        value = dot(turned, zh_ref[...]) + dot(turned, zl_ref[...])
+        value = dot(jnp.concatenate([turned, turned], axis=1), z_ref[...])
         out_ref[jnp.where(flip_ref[0] == 1, span - 1 - i, i)] = value
 
 
-def volume_call(flip, data, restore, table_z):
-    slabs, slab, width, grid = data.shape
+def volume_call(flip, parts, restore, table_z):
+    slabs, slab, width, grid = parts[0].shape
     span = 4
     steps = slab // span
     fixed = lambda i, flip_ref: (0, 0)
@@ -435,12 +463,8 @@
         grid_spec=pltpu.PrefetchScalarGridSpec(
             num_scalar_prefetch=1,
             grid=(steps,),
-            in_specs=[
-                pl.BlockSpec((slabs, span, width, grid), lambda i, flip_ref: (0, i, 0, 0)),
-                pl.BlockSpec(restore.shape, fixed),
-                pl.BlockSpec(table_z[0].shape, fixed),
-                pl.BlockSpec(table_z[1].shape, fixed),
-            ],
+            in_specs=[pl.BlockSpec(restore.shape, fixed), pl.BlockSpec(table_z.shape, fixed)]
+            + [pl.BlockSpec((slabs, span, width, grid), lambda i, flip_ref: (0, i, 0, 0))] * len(parts),
             out_specs=pl.BlockSpec(
                 (span, grid, grid), lambda i, flip_ref: (jnp.where(flip_ref[0] == 1, steps - 1 - i, i), 0, 0)
             ),
@@ -448,7 +472,7 @@
         out_shape=jax.ShapeDtypeStruct((slab, grid, grid), F32),
         compiler_params=pltpu.CompilerParams(vmem_limit_bytes=48 * 2**20),
         name="volume",
-    )(flip, data, restore, *table_z)
+    )(flip, restore, table_z, *parts)
 
 
 def sorted_points(interp_cells, grid):
@@ -458,24 +482,10 @@
     row = (base // grid + 1) & (grid - 1)
     key = row * points + jnp.arange(points, dtype=jnp.int32)
     key = lax.sort(key, is_stable=False)
-    rows = jnp.arange(grid, dtype=jnp.int32)
-    count = jnp.sum((row[None, :] == rows[:, None]).astype(jnp.int32), axis=1)
-    first = jnp.cumsum(count) - count
-    chunks = jnp.maximum((count + (CHUNK - 1)) // CHUNK, 1)
-    ends = jnp.cumsum(chunks)
-    most = grid + points // CHUNK + UNROLL + 1
-    number = jnp.arange(most, dtype=jnp.int32)
-    chunk_row = jnp.minimum(jnp.sum((ends[None, :] <= number[:, None]).astype(jnp.int32), axis=1), grid - 1)
-    mine = (rows[None, :] == chunk_row[:, None]).astype(jnp.int32)
-    shift = first - (ends - chunks) * CHUNK
-    chunk_start = jnp.sum(mine * shift[None, :], axis=1) + number * CHUNK
-    row_end = jnp.sum(mine * (first + count)[None, :], axis=1)
-    used = number < ends[-1]
-    chunk_size = jnp.where(used, jnp.clip(row_end - chunk_start, 0, CHUNK), 0)
-    chunk_start = jnp.where(used, chunk_start, points)
-    turns = ((ends[-1] + (UNROLL - 1)) // UNROLL).reshape(1)
+    rows = jnp.arange(grid + 3, dtype=jnp.int32)
+    first = jnp.sum((row[None, :] < rows[:, None]).astype(jnp.int32), axis=1)
     point = jnp.concatenate([key & (points - 1), jnp.zeros((CHUNK,), jnp.int32)])
-    return turns, chunk_row, chunk_start, chunk_size, point
+    return first, point
 
 
 def arrange_kernel(rows_ref, eye_ref, order_ref, kept_ref, sent_ref, *lines):
@@ -585,8 +595,10 @@
     own = lax.axis_index("vol")
     single = (own == slab_count // 2).astype(jnp.int32).reshape(1)
     flip = (own >= slab_count // 2).astype(jnp.int32).reshape(1)
-    sent = planes_call(single, plane, table_y, table_x, slab_count, grid)
-    received = lax.all_to_all(sent, "vol", split_axis=0, concat_axis=0, tiled=True)
+    received = []
+    for part in range(max(1, slab // STEP)):
+        sent = planes_call(single, plane, table_y, table_x, slab_count, grid, part)
+        received.append(lax.all_to_all(sent, "vol", split_axis=0, concat_axis=0, tiled=True))
     return volume_call(flip, received, restore, table_z)[None]
 
 

time: 324 us -> 311 us (0.960)
  waiting for transfers between devices: 97.2 us -> 87.4 us
  starting transfers between devices: 19.8 us -> 23.3 us
    all_to_all x1 -> x2, waiting for transfers between devices: 49.1 us -> 38.8 us  [shards(): lax.all_to_all(sent, 'vol', split_axis=0, concat_axis=0, tiled=True)]
    pallas_call x1, Pallas kernels: 80.9 us -> 73.2 us  [scatter_call(): pl.pallas_call(functools.partial(scatter_kernel, cap, width, grid), out_s...]
    pallas_call x1 -> x2, Pallas kernels: 23 us -> 28.3 us  [planes_call(): pl.pallas_call(functools.partial(plane_kernel, slabs, grid, final), grid_...]
    all_to_all x1 -> x2, starting transfers between devices: 4.69 us -> 8.2 us  [shards(): lax.all_to_all(sent, 'vol', split_axis=0, concat_axis=0, tiled=True)]
  transfers between devices with their start and end apart: 5 -> 6, of which waited for: 3 -> 4; matrix products, arithmetic and copies ran while one was open for 14% -> 15% of each run, Pallas kernels for 9% -> 14%
where the time goes in v1:
time: 311 us; the launch traced here: 309 us
  Pallas kernels  147 us (47%)
  waiting for transfers between devices  87.4 us (28%)
  local copies, waits for them, and re-layouts  29.1 us (9%)
  starting transfers between devices  23.3 us (7%)
  other arithmetic  21.9 us (7%)
    pallas_call x1, Pallas kernels, scatter_call(): pl.pallas_call(functools.partial(scatter_kernel, cap, width, grid), out_s...  73.2 us
    ppermute x1, waiting for transfers between devices, paired_rows(): lax.ppermute(sent, 'vol', [(i, slabs - 1 - i) for i in range(slabs)])  39 us
    all_to_all x2, waiting for transfers between devices, shards(): lax.all_to_all(sent, 'vol', split_axis=0, concat_axis=0, tiled=True)  38.8 us
    pallas_call x2, Pallas kernels, planes_call(): pl.pallas_call(functools.partial(plane_kernel, slabs, grid, final), grid_...  28.3 us
    pallas_call x1, Pallas kernels, arrange_call(): pl.pallas_call(arrange_kernel, out_shape=(shape, shape), in_specs=[vmem]...  21.4 us
    all_to_all x1, waiting for transfers between devices, shards(): lax.all_to_all(copies, 'vol', split_axis=0, concat_axis=0, tiled=True)  9.67 us
    pallas_call x1, Pallas kernels, volume_call(): pl.pallas_call(volume_kernel, grid_spec=pltpu.PrefetchScalarGridSpec(num_...  9.62 us
    all_to_all x2, starting transfers between devices, shards(): lax.all_to_all(sent, 'vol', split_axis=0, concat_axis=0, tiled=True)  8.2 us
  transfers between devices with their start and end apart: 6, of which 4 were waited for; matrix products, arithmetic and copies ran while one was open for 15% of the time, Pallas kernels for 14%

profile of v1, /device:TPU:0, one launch (start us, length us, event | category | flops | bytes accessed | tf_op | source)
XLA Modules:
  0.0 308.9 jit_solution(16098832528776862968)
XLA Ops:
  0.0 1.0 slice_bitcast_fusion
  1.0 4.9 %collective-permute-start = (bf16[128,1,2,256]{3,2,1,0:T(2,128)(2,1)S(1)}, bf16[128,1,2,256]{3,2,1,0:T(2,128)(2,1)S(1)}, u32[]{:S(2)}, u32[]{:S(2)}) collective-permute-start(bf16[128,1,2,256]{3,2,1,0:T(2,128)(2,1)S(1)} %slice_bitcast_fusion), channel_id=1, source_target_pairs={{0,4},{1,0},{2,1},{3,2},{4,3},{8,12},{9,8},{10,9},{11,10},{12,11},... | collective-permute-start | bytes 393224 | tf_op jit(solution)/shard_map/ppermute | solution.py:576
  5.9 0.7 copy.25.classes_ref
  6.6 1.6 copy-done
  8.2 1.0 copy-done.1
  9.3 0.9 copy-done.2
  10.2 7.1 %route.1 = bf16[32,32,16,128]{3,2,1,0:T(8,128)(2,1)} custom-call(s32[8,1]{1,0:T(8,128)S(1)} %copy.25.classes_ref, bf16[8,256,2,256]{3,2,1,0:T(2,128)(2,1)S(1)} %copy-done, bf16[256,256]{1,0:T(8,128)(2,1)S(1)} %copy-done.2, bf16[512,512]{1,0:T(8,128)(2,1)S(1)} %copy-done.1), custom_call_target="tpu_custom_call" | custom-call | tf_op jit(solution)/shard_map/route/pallas_call | solution.py:132
  17.2 0.0 collective-permute-done
  17.2 4.4 %all-to-all-start = ((bf16[32,32,16,128]{3,2,1,0:T(8,128)(2,1)}), bf16[32,32,16,128]{3,2,1,0:T(8,128)(2,1)}, u32[]{:S(2)}, u32[]{:S(2)}) async-start(bf16[32,32,16,128]{3,2,1,0:T(8,128)(2,1)} %route.1), calls=%async_computation | async-start | bytes 8388608 | tf_op jit(solution)/shard_map/all_to_all | solution.py:578
  21.7 0.0 slice-done
  21.7 0.1 copy.35
  21.8 0.0 copy-done.7
  21.8 0.0 copy-done.8
  21.8 4.9 %slice.18 = bf16[128,31,2,256]{3,2,1,0:T(2,128)(2,1)S(1)} slice(bf16[128,32,2,256]{3,2,1,0:T(2,128)(2,1)} %bitcast.23), slice={[0:128], [1:32], [0:2], [0:256]} | slice | bytes 8126464 | tf_op jit(solution)/shard_map/slice | solution.py:552
  26.8 1.0 broadcast_select_fusion
  27.8 0.0 copy-start.3
  27.8 7.4 %pad_maximum_fusion.rows_ref = bf16[128,32,2,256]{3,2,1,0:T(2,128)(2,1)} fusion(bf16[128,31,2,256]{3,2,1,0:T(2,128)(2,1)S(1)} %slice.18, bf16[128,1,2,256]{3,2,1,0:T(2,128)(2,1)S(1)} %broadcast_select_fusion), kind=kLoop, calls=%fused_computation.2 | loop fusion | flops 2097152 | bytes 8388608 | tf_op jit(solution)/shard_map/concatenate | solution.py:552
  35.2 0.0 copy-done.3
  35.3 21.4 %arrange.1 = (bf16[16,512,128]{2,1,0:T(8,128)(2,1)S(1)}, bf16[16,512,128]{2,1,0:T(8,128)(2,1)}) custom-call(bf16[128,32,2,256]{3,2,1,0:T(2,128)(2,1)} %pad_maximum_fusion.rows_ref, bf16[256,256]{1,0:T(8,128)(2,1)S(1)} %copy-done.3, bf16[256,256]{1,0:T(8,128)(2,1)S(1)} %broadcast_select_fusion.1.order_ref), custom_call_target="tpu_custom_call" | custom-call | tf_op jit(solution)/shard_map/arrange/pallas_call | solution.py:521
  56.7 2.3 collective-permute-start.1
  59.0 0.1 iota_add_fusion
  59.1 7.3 %sort.7 = s32[32768]{0:T(1024)S(1)} sort(s32[32768]{0:T(1024)S(1)} %get-tuple-element.27), dimensions={0}, to_apply=%region_1.2 | sort | flops 491520 | bytes 262144 | tf_op jit(solution)/shard_map/sort | solution.py:484
  66.4 1.3 copy.28
  67.7 0.1 pad.8.clone
  67.8 0.1 and_convert_fusion
  67.9 0.2 maximum_maximum_fusion
  68.2 1.3 copy.29
  69.4 1.6 reshape.58
  71.1 4.6 %copy.30 = f32[32,512,16]{2,1,0:T(8,128)} copy(f32[32,512,16]{1,2,0:T(8,128)S(1)} %reshape.58) | data formatting | bytes 2097152 | tf_op jit(solution)/shard_map/reshape | solution.py:584
  75.7 7.6 %pad.5.weights_ref = f32[32,512,128]{2,1,0:T(8,128)} pad(f32[32,512,16]{2,1,0:T(8,128)} %copy.30, f32[]{:T(128)} %constant.21.clone.1), padding=0_0x0_0x0_112 | pad | bytes 9437188 | tf_op jit(solution)/shard_map/jit(_pad)/pad | solution.py:585
  83.3 0.7 concatenate.11.point_ref
  84.0 5.6 %convert_reduce_fusion.first_ref = s32[259]{0:T(512)} fusion(s32[32768]{0:T(1024)S(1)} %get-tuple-element.28), kind=kLoop, calls=%fused_computation | loop fusion | flops 25460476 | bytes 132108 | tf_op jit(solution)/shard_map/reduce_sum | solution.py:486
  89.6 39.0 %collective-permute-done.1.joined_ref = bf16[16,512,128]{2,1,0:T(8,128)(2,1)} collective-permute-done((bf16[16,512,128]{2,1,0:T(8,128)(2,1)}, bf16[16,512,128]{2,1,0:T(8,128)(2,1)}, u32[]{:S(2)}, u32[]{:S(2)}) %collective-permute-start.1) | collective-permute-done | bytes 2097184 | tf_op jit(solution)/shard_map/ppermute | solution.py:556
  128.6 0.0 all-to-all-done.images_ref
  128.6 7.3 %scores.1 = f32[128,128]{1,0:T(8,128)S(1)} custom-call(bf16[32,32,16,128]{3,2,1,0:T(8,128)(2,1)} %all-to-all-done.images_ref, bf16[16,512,128]{2,1,0:T(8,128)(2,1)S(1)} %get-tuple-element.24.kept_ref, bf16[16,512,128]{2,1,0:T(8,128)(2,1)} %collective-permute-done.1.joined_ref), custom_call_target="tpu_custom_call" | custom-call | tf_op jit(solution)/shard_map/scores/pallas_call | solution.py:179
  136.0 0.8 broadcast_in_dim.7
  136.8 3.5 %all-to-all-start.1 = ((f32[8,128,128]{2,1,0:T(8,128)}), f32[8,128,128]{2,1,0:T(8,128)S(1)}, u32[]{:S(2)}, u32[]{:S(2)}) async-start(f32[8,128,128]{2,1,0:T(8,128)} %broadcast_in_dim.7), calls=%async_computation.1 | async-start | bytes 1048576 | tf_op jit(solution)/shard_map/all_to_all | solution.py:592
  140.3 9.7 %all-to-all-done.1.parts_ref = f32[8,128,128]{2,1,0:T(8,128)S(1)} async-done(((f32[8,128,128]{2,1,0:T(8,128)}), f32[8,128,128]{2,1,0:T(8,128)S(1)}, u32[]{:S(2)}, u32[]{:S(2)}) %all-to-all-start.1) | async-done | bytes 524320 | tf_op jit(solution)/shard_map/all_to_all | solution.py:592
  150.0 0.8 copy-done.6
  150.8 73.2 %scatter.1 = f32[2,16896,128]{2,1,0:T(8,128)} custom-call(s32[259]{0:T(512)} %convert_reduce_fusion.first_ref, s32[32896]{0:T(1024)} %concatenate.11.point_ref, f32[8,128,128]{2,1,0:T(8,128)} %copy-done.6, bf16[32,32,16,128]{3,2,1,0:T(8,128)(2,1)} %all-to-all-done.images_ref, f32[32,512,128]{2,1,0:T(8,128)} %pad.5.weights_ref), custom_call_target="tpu_custom_call" | custom-call | tf_op jit(solution)/shard_map/scatter/pallas_call | solution.py:338
  224.0 14.1 %planes.3 = bf16[8,32,16,256]{3,2,1,0:T(8,128)(2,1)} custom-call(s32[1]{0:T(128)} %bitcast.1.flag_ref, f32[2,2,32,264,128]{4,3,2,1,0:T(8,128)} %bitcast.21, bf16[768,256]{1,0:T(8,128)(2,1)} %constant.54.clone.y_ref, bf16[272,768]{1,0:T(8,128)(2,1)} %constant.55.clone.x_ref), custom_call_target="tpu_custom_call" | custom-call | tf_op jit(solution)/shard_map/planes/pallas_call | solution.py:427
  238.1 3.9 %all-to-all-start.3 = ((bf16[8,32,16,256]{3,2,1,0:T(8,128)(2,1)}), bf16[8,32,16,256]{3,2,1,0:T(8,128)(2,1)S(1)}, u32[]{:S(2)}, u32[]{:S(2)}) async-start(bf16[8,32,16,256]{3,2,1,0:T(8,128)(2,1)} %planes.3), calls=%async_computation.3 | async-start | bytes 4194304 | tf_op jit(solution)/shard_map/all_to_all | solution.py:601
  242.0 14.2 %planes.2 = bf16[8,32,16,256]{3,2,1,0:T(8,128)(2,1)} custom-call(s32[1]{0:T(128)} %bitcast.1.flag_ref, f32[2,2,32,264,128]{4,3,2,1,0:T(8,128)} %bitcast.22, bf16[768,256]{1,0:T(8,128)(2,1)} %constant.54.clone.y_ref, bf16[272,768]{1,0:T(8,128)(2,1)} %constant.55.clone.x_ref), custom_call_target="tpu_custom_call" | custom-call | tf_op jit(solution)/shard_map/planes/pallas_call | solution.py:427
  256.2 12.1 %all-to-all-done.3.refs_1_ = bf16[8,32,16,256]{3,2,1,0:T(8,128)(2,1)S(1)} async-done(((bf16[8,32,16,256]{3,2,1,0:T(8,128)(2,1)}), bf16[8,32,16,256]{3,2,1,0:T(8,128)(2,1)S(1)}, u32[]{:S(2)}, u32[]{:S(2)}) %all-to-all-start.3) | async-done | bytes 2097184 | tf_op jit(solution)/shard_map/all_to_all | solution.py:601
  268.3 4.3 %all-to-all-start.2 = ((bf16[8,32,16,256]{3,2,1,0:T(8,128)(2,1)}), bf16[8,32,16,256]{3,2,1,0:T(8,128)(2,1)}, u32[]{:S(2)}, u32[]{:S(2)}) async-start(bf16[8,32,16,256]{3,2,1,0:T(8,128)(2,1)} %planes.2), calls=%async_computation.2 | async-start | bytes 4194304 | tf_op jit(solution)/shard_map/all_to_all | solution.py:601
  272.6 26.6 %all-to-all-done.2.refs_0_ = bf16[8,32,16,256]{3,2,1,0:T(8,128)(2,1)} async-done(((bf16[8,32,16,256]{3,2,1,0:T(8,128)(2,1)}), bf16[8,32,16,256]{3,2,1,0:T(8,128)(2,1)}, u32[]{:S(2)}, u32[]{:S(2)}) %all-to-all-start.2) | async-done | bytes 2097184 | tf_op jit(solution)/shard_map/all_to_all | solution.py:601
  299.3 0.0 copy-done.4
  299.3 9.6 %volume.1 = f32[32,256,256]{2,1,0:T(8,128)} custom-call(s32[1]{0:T(128)} %bitcast.flip_ref, bf16[256,256]{1,0:T(8,128)(2,1)S(1)} %copy-done.5, bf16[512,256]{1,0:T(8,128)(2,1)S(1)} %copy-done.4, bf16[8,32,16,256]{3,2,1,0:T(8,128)(2,1)} %all-to-all-done.2.refs_0_, bf16[8,32,16,256]{3,2,1,0:T(8,128)(2,1)S(1)} %all-to-all-done.3.refs_1_), custom_call_target="tpu_custom_call" | custom-call | tf_op jit(solution)/shard_map/volume/pallas_call | solution.py:461
  (13 shorter events, 0.0 us)
Async XLA Ops:
  1.0 16.2 %collective-permute-start = (bf16[128,1,2,256]{3,2,1,0:T(2,128)(2,1)S(1)}, bf16[128,1,2,256]{3,2,1,0:T(2,128)(2,1)S(1)}, u32[]{:S(2)}, u32[]{:S(2)}) collective-permute-start(bf16[128,1,2,256]{3,2,1,0:T(2,128)(2,1)S(1)} %slice_bitcast_fusion), channel_id=1, source_target_pairs={{0,4},{1,0},{2,1},{3,2},{4,3},{8,12},{9,8},{10,9},{11,10},{12,11},... | collective-permute-start | bytes 393224 | tf_op jit(solution)/shard_map/ppermute | solution.py:576
  6.6 1.6 copy-start
  8.2 1.0 copy-start.1
  9.2 0.9 copy-start.2
  17.2 4.4 %slice-start = ((s32[128,4,256]{2,1,0:T(4,128)}), s32[128,1,256]{2,1,0:T(1,128)S(1)}, s32[]{:S(2)}) async-start(s32[128,4,256]{2,1,0:T(4,128)} %param.16), calls=%async_computation.4 | async-start | bytes 262144 | tf_op jit(solution)/shard_map/slice | solution.py:581
  17.2 4.6 %copy-start.7 = (bf16[256,256]{1,0:T(8,128)(2,1)S(1)}, bf16[256,256]{1,0:T(8,128)(2,1)}, u32[]{:S(2)}) copy-start(bf16[256,256]{1,0:T(8,128)(2,1)} %constant.52.clone) | copy-start | bytes 393220
  17.2 4.6 %copy-start.8 = (bf16[256,256]{1,0:T(8,128)(2,1)S(1)}, bf16[256,256]{1,0:T(8,128)(2,1)}, u32[]{:S(2)}) copy-start(bf16[256,256]{1,0:T(8,128)(2,1)} %constant.53.clone) | copy-start | bytes 393220
  17.2 111.4 %all-to-all-start = ((bf16[32,32,16,128]{3,2,1,0:T(8,128)(2,1)}), bf16[32,32,16,128]{3,2,1,0:T(8,128)(2,1)}, u32[]{:S(2)}, u32[]{:S(2)}) async-start(bf16[32,32,16,128]{3,2,1,0:T(8,128)(2,1)} %route.1), calls=%async_computation | async-start | bytes 8388608 | tf_op jit(solution)/shard_map/all_to_all | solution.py:578
  27.8 7.4 %copy-start.3 = (bf16[256,256]{1,0:T(8,128)(2,1)S(1)}, bf16[256,256]{1,0:T(8,128)(2,1)}, u32[]{:S(2)}) copy-start(bf16[256,256]{1,0:T(8,128)(2,1)} %constant.50.clone.eye_ref) | copy-start | bytes 393220
  56.7 71.9 %collective-permute-start.1 = (bf16[16,512,128]{2,1,0:T(8,128)(2,1)}, bf16[16,512,128]{2,1,0:T(8,128)(2,1)}, u32[]{:S(2)}, u32[]{:S(2)}) collective-permute-start(bf16[16,512,128]{2,1,0:T(8,128)(2,1)} %get-tuple-element.20), channel_id=1, source_target_pairs={{0,7},{1,6},{2,5},{3,4},{4,3},{5,2},{6,1},{7,0},{8,15},{9,14},{10,... | collective-permute-start | bytes 6291464 | tf_op jit(solution)/shard_map/ppermute | solution.py:556
  136.8 13.2 %all-to-all-start.1 = ((f32[8,128,128]{2,1,0:T(8,128)}), f32[8,128,128]{2,1,0:T(8,128)S(1)}, u32[]{:S(2)}, u32[]{:S(2)}) async-start(f32[8,128,128]{2,1,0:T(8,128)} %broadcast_in_dim.7), calls=%async_computation.1 | async-start | bytes 1048576 | tf_op jit(solution)/shard_map/all_to_all | solution.py:592
  150.0 0.8 copy-start.6
  238.1 30.2 %all-to-all-start.3 = ((bf16[8,32,16,256]{3,2,1,0:T(8,128)(2,1)}), bf16[8,32,16,256]{3,2,1,0:T(8,128)(2,1)S(1)}, u32[]{:S(2)}, u32[]{:S(2)}) async-start(bf16[8,32,16,256]{3,2,1,0:T(8,128)(2,1)} %planes.3), calls=%async_computation.3 | async-start | bytes 4194304 | tf_op jit(solution)/shard_map/all_to_all | solution.py:601
  256.2 43.1 %copy-start.4 = (bf16[512,256]{1,0:T(8,128)(2,1)S(1)}, bf16[512,256]{1,0:T(8,128)(2,1)}, u32[]{:S(2)}) copy-start(bf16[512,256]{1,0:T(8,128)(2,1)} %constant.57.clone.z_ref) | copy-start | bytes 786436
  256.2 43.1 %copy-start.5 = (bf16[256,256]{1,0:T(8,128)(2,1)S(1)}, bf16[256,256]{1,0:T(8,128)(2,1)}, u32[]{:S(2)}) copy-start(bf16[256,256]{1,0:T(8,128)(2,1)} %constant.56.clone.restore_ref) | copy-start | bytes 393220
  268.3 31.0 %all-to-all-start.2 = ((bf16[8,32,16,256]{3,2,1,0:T(8,128)(2,1)}), bf16[8,32,16,256]{3,2,1,0:T(8,128)(2,1)}, u32[]{:S(2)}, u32[]{:S(2)}) async-start(bf16[8,32,16,256]{3,2,1,0:T(8,128)(2,1)} %planes.2), calls=%async_computation.2 | async-start | bytes 4194304 | tf_op jit(solution)/shard_map/all_to_all | solution.py:601
